TPU v7x, 32 devices: a whole 2x2x4 slice. The times are simulated.
32 devices in a mesh: lev: 2 (over x), hor: 16 (over z, y, core).
Axes of the slice: x: 2, y: 2, z: 4, core: 2. Of those that a mesh axis runs over, the one named last changes fastest.
Arguments:
- slab_fields: float32 [4, 32, 65536], P(None, 'lev', 'hor'), may hold values from -6 to 6
- sample_index: int32 [16, 256], P('hor', 'lev'), may hold values from 0 to 2047
- thickness: float32 [32], replicated, may hold values from 0.3 to 3
- level_cuts: int32 [31], replicated, may hold values 0 or 1
Outputs:
- gram: float32 [2176, 2176], P('hor', 'lev')
Inputs may be any that keep to these rules, and one draw needn't show every extreme that they name: sample_index[j, k] indexes a column among the 2048 columns that start at j * 4096 + (k // 128) * 2048.
All inputs are finite; a program needn't handle non-finite values.
Results may differ from a plain program's by a relative error of at most 0.00068.
Values may be sent and summed in bfloat16 or wider, within the bound.
A program may use at most 128 MiB of HBM per device.

v0:
```python
import jax
import jax.numpy as jnp
from jax import lax
from jax.sharding import PartitionSpec as P


def vertical_filter(values, thickness, level_cuts):
    link = 1.0 - level_cuts.astype(jnp.float32)
    zero_one = jnp.zeros((1,), jnp.float32)
    lower_link = jnp.concatenate([zero_one, link])
    upper_link = jnp.concatenate([link, zero_one])
    lower_weight = jnp.concatenate([zero_one, thickness[:-1]]) * lower_link
    upper_weight = jnp.concatenate([thickness[1:], zero_one]) * upper_link
    zero_row = jnp.zeros_like(values[:, :1, :])
    below = jnp.concatenate([zero_row, values[:, :-1, :]], axis=1)
    above = jnp.concatenate([values[:, 1:, :], zero_row], axis=1)
    numer = (
        2.0 * thickness[None, :, None] * values
        + lower_weight[None, :, None] * below
        + upper_weight[None, :, None] * above
    )
    denom = 2.0 * thickness + lower_weight + upper_weight
    return numer / denom[None, :, None]


def quadratic_features(smooth):
    count = smooth.shape[2]
    later = jnp.concatenate([smooth[2], smooth[3]], axis=0)
    earlier = jnp.concatenate([smooth[0], smooth[1]], axis=0)
    product = (later[:, None, :] * smooth[0][None, :, :]).reshape(-1, count)
    return jnp.concatenate([later, earlier, product], axis=0).astype(jnp.bfloat16)


def on_device(slab_fields, sample_index, thickness, level_cuts):
    samp_count = sample_index.shape[1]
    lev_count = lax.axis_size("lev")
    hor_count = lax.axis_size("hor")
    all_lists = lax.all_gather(sample_index, "lev", axis=1, tiled=True)[0]
    group_cols = slab_fields.shape[2] // lev_count
    offsets = jnp.arange(all_lists.shape[0]) // samp_count * group_cols + all_lists
    chosen = jnp.take(slab_fields, offsets, axis=2)
    picked_cols = lax.all_to_all(chosen, "lev", split_axis=2, concat_axis=1, tiled=True)
    smooth = vertical_filter(picked_cols, thickness, level_cuts)
    feat_count = 4 * smooth.shape[1] + 2 * smooth.shape[1] * smooth.shape[1]
    col_count = feat_count // lev_count
    col_start = lax.axis_index("lev") * col_count
    features_bf = quadratic_features(smooth)
    block_features_bf = lax.all_gather(features_bf, "lev", axis=1, tiled=True)
    chosen_rows = lax.dynamic_slice_in_dim(block_features_bf, col_start, col_count, 0)
    column_block = lax.dot_general(
        block_features_bf, chosen_rows, (((1,), (1,)), ((), ())), preferred_element_type=jnp.float32
    )
    gram_block = lax.psum_scatter(column_block, "hor", scatter_dimension=0, tiled=True)
    count_all = samp_count * lev_count * hor_count
    return gram_block / count_all


def solution(mesh):
    in_specs = (P(None, "lev", "hor"), P("hor", "lev"), P(), P())
    out_specs = P("hor", "lev")
    return jax.shard_map(
        on_device, mesh=mesh, in_specs=in_specs, out_specs=out_specs, check_vma=False
    )
```

profile of v0, /device:TPU:0, one launch (start us, length us, event | category | flops | bytes accessed | tf_op | source)
XLA Modules:
  0.0 190.3 jit_solution(6274469803172797929)
XLA Ops:
  6.5 5.3 %all_gather.6 = s32[1,256]{1,0:T(1,128)S(1)} all-gather(s32[1,128]{1,0:T(1,128)} %param.5), channel_id=1, replica_groups=mesh['lev'=2,'hor'=16] {'lev'}, dimensions={1}, use_global_device_ids=true | all-gather | bytes 1536 | tf_op jit(solution)/shard_map/all_gather | solution.py:38
  11.9 6.9 %copy.7 = f32[4,16,4096]{1,0,2:T(4,128)} copy(f32[4,16,4096]{2,1,0:T(8,128)} %param.4) | data formatting | bytes 2097152 | tf_op args[0]
  18.8 0.0 copy-start.1
  18.8 0.0 copy-start.2
  18.8 4.4 %gather_fusion = f32[256,4,16]{2,1,0:T(4,128)S(1)} fusion(f32[4,16,4096]{1,0,2:T(4,128)} %copy.7, s32[1024]{0:T(1024)S(1)} %pad_clamp_fusion), kind=kCustom, calls=%fused_computation | custom fusion | bytes 132096 | tf_op jit(solution)/shard_map/jit(_take)/gather | solution.py:41
  23.2 0.3 fusion.14
  23.5 1.1 reshape.135
  24.6 3.3 %all-to-all-start = ((f32[2,1,8192]{2,1,0:T(1,128)}), f32[2,1,8192]{2,1,0:T(1,128)S(1)}, u32[]{:S(2)}, u32[]{:S(2)}) async-start(f32[2,1,8192]{2,1,0:T(1,128)} %reshape.135), calls=%async_computation | async-start | bytes 131072 | tf_op jit(solution)/shard_map/all_to_all | solution.py:42
  27.9 0.0 all-gather.2.cloned.1.call-start
  28.0 0.0 copy-done.1
  28.0 0.0 copy-done.2
  28.0 0.1 fusion.13
  28.0 0.1 add_add_fusion
  28.1 3.9 %all-to-all-done = f32[2,1,8192]{2,1,0:T(1,128)S(1)} async-done(((f32[2,1,8192]{2,1,0:T(1,128)}), f32[2,1,8192]{2,1,0:T(1,128)S(1)}, u32[]{:S(2)}, u32[]{:S(2)}) %all-to-all-start) | async-done | bytes 65568 | tf_op jit(solution)/shard_map/all_to_all | solution.py:42
  32.0 0.5 broadcast.122
  32.5 0.8 reduce
  33.4 0.4 reshape.136
  33.8 0.2 copy.8
  34.0 0.1 add_divide_fusion
  34.1 0.1 multiply_convert_fusion
  34.2 0.1 constant_dynamic-update-slice_fusion
  34.3 0.0 copy-start
  34.3 0.8 copy-done
  35.1 0.0 all-gather.2.cloned.1.call-update
  35.2 0.0 reduce-scatter.4.cloned.1.call-start
  35.2 22.9 %all-gather.2.cloned.1.call-done = bf16[2176,256]{1,0:T(8,128)(2,1)} async-done(((bf16[2176,128]{1,0:T(8,128)(2,1)}), bf16[2176,256]{1,0:T(8,128)(2,1)}) %all-gather.2.cloned.1.call-update) | async-done | bytes 1114128 | tf_op jit(solution)/shard_map/all_gather | solution.py:48
  58.1 6.8 %fusion = f32[2176,1088]{1,0:T(8,128)} fusion(bf16[2176,256]{1,0:T(8,128)(2,1)} %all-gather.2.cloned.1.call-done, s32[]{:T(128)S(6)} %select_n.43), kind=kOutput, calls=%fused_computation.2 | convolution fusion | flops 1212153856 | bytes 11141124 | tf_op jit(solution)/shard_map/dot_general | solution.py:50
  65.0 0.0 reduce-scatter.4.cloned.1.call-update
  65.0 116.5 %reduce-scatter.4.cloned.1.call-done = f32[136,1088]{1,0:T(8,128)} async-done(((f32[2176,1088]{1,0:T(8,128)}), f32[136,1088]{1,0:T(8,128)}) %reduce-scatter.4.cloned.1.call-update) | async-done | bytes 591888
  181.5 1.9 %broadcast_multiply_fusion = f32[136,1088]{1,0:T(8,128)} fusion(f32[136,1088]{1,0:T(8,128)} %reduce-scatter.4.cloned.1.call-done), kind=kLoop, calls=%fused_computation.5 | loop fusion | flops 147968 | bytes 1183744 | tf_op jit(solution)/shard_map/div | solution.py:55
  (10 shorter events, 0.1 us)
Async XLA Ops:
  18.8 9.2 %copy-start.1 = (f32[32]{0:T(128)S(1)}, f32[32]{0:T(128)}, u32[]{:S(2)}) copy-start(f32[32]{0:T(128)} %param.6) | copy-start | bytes 388
  18.8 9.2 %copy-start.2 = (s32[31]{0:T(128)S(1)}, s32[31]{0:T(128)}, u32[]{:S(2)}) copy-start(s32[31]{0:T(128)} %param.7) | copy-start | bytes 376
  24.6 7.4 %all-to-all-start = ((f32[2,1,8192]{2,1,0:T(1,128)}), f32[2,1,8192]{2,1,0:T(1,128)S(1)}, u32[]{:S(2)}, u32[]{:S(2)}) async-start(f32[2,1,8192]{2,1,0:T(1,128)} %reshape.135), calls=%async_computation | async-start | bytes 131072 | tf_op jit(solution)/shard_map/all_to_all | solution.py:42
  27.9 30.2 %all-gather.2.cloned.1.call-start = ((), (), s32[]{:S(2)}) async-start(), calls=%async_computation.2 | async-start | bytes 1671168 | tf_op jit(solution)/shard_map/all_gather | solution.py:48
  34.3 0.8 copy-start
  35.2 146.3 %reduce-scatter.4.cloned.1.call-start = ((), (), s32[]{:S(2)}) async-start(), calls=%async_computation.3 | async-start | bytes 10653696
Sparse Core Ops, SparseCore 0:
  35.3 22.8 all-gather.1
  65.1 116.3 reduce-scatter.3
where the time goes:
time: 191 us; the launch traced here: 190 us
  waiting for transfers between devices  143 us (75%)
  local copies, waits for them, and re-layouts  14.4 us (8%)
  between operations  13.6 us (7%)
  matrix products  6.84 us (4%)
  blocking collectives  5.3 us (3%)
  other arithmetic  3.49 us (2%)
  starting transfers between devices  3.38 us (2%)
    unnamed x3, waiting for transfers between devices  117 us
    all_gather x1, waiting for transfers between devices, on_device(): block_features_bf = lax.all_gather(features_bf, 'lev', axis=1, tiled=True)  22.9 us
    unnamed x13, local copies, waits for them, and re-layouts  9.19 us
    dot_general x1, matrix products, on_device(): lax.dot_general(block_features_bf, chosen_rows, (((1,), (1,)), ((), ())),...  6.84 us
    all_gather x1, blocking collectives, on_device(): all_lists = lax.all_gather(sample_index, 'lev', axis=1, tiled=True)[0]  5.3 us
    gather x1, local copies, waits for them, and re-layouts, on_device(): chosen = jnp.take(slab_fields, offsets, axis=2)  4.42 us
    all_to_all x1, waiting for transfers between devices, on_device(): lax.all_to_all(chosen, 'lev', split_axis=2, concat_axis=1, tiled=True)  3.88 us
  transfers between devices with their start and end apart: 3, of which 3 were waited for; matrix products, arithmetic and copies ran while one was open for 0% of the time, Pallas kernels for 0%

commit v1 on v0

--- a/solution.py
+++ b/solution.py
@@ -1,16 +1,25 @@
 import jax
 import jax.numpy as jnp
 from jax import lax
+from jax.experimental import pallas as pl
+from jax.experimental.pallas import tpu as pltpu
 from jax.sharding import PartitionSpec as P
 
-
-def vertical_filter(values, thickness, level_cuts):
+MESH = pl.DeviceIdType.MESH
+
+
+def filter_weights(thickness, level_cuts):
     link = 1.0 - level_cuts.astype(jnp.float32)
     zero_one = jnp.zeros((1,), jnp.float32)
     lower_link = jnp.concatenate([zero_one, link])
     upper_link = jnp.concatenate([link, zero_one])
     lower_weight = jnp.concatenate([zero_one, thickness[:-1]]) * lower_link
     upper_weight = jnp.concatenate([thickness[1:], zero_one]) * upper_link
+    return lower_weight, upper_weight
+
+
+def vertical_filter(values, thickness, level_cuts):
+    lower_weight, upper_weight = filter_weights(thickness, level_cuts)
     zero_row = jnp.zeros_like(values[:, :1, :])
     below = jnp.concatenate([zero_row, values[:, :-1, :]], axis=1)
     above = jnp.concatenate([values[:, 1:, :], zero_row], axis=1)
@@ -31,7 +40,7 @@
     return jnp.concatenate([later, earlier, product], axis=0).astype(jnp.bfloat16)
 
 
-def on_device(slab_fields, sample_index, thickness, level_cuts):
+def general_plan(slab_fields, sample_index, thickness, level_cuts):
     samp_count = sample_index.shape[1]
     lev_count = lax.axis_size("lev")
     hor_count = lax.axis_size("hor")
@@ -55,9 +64,215 @@
     return gram_block / count_all
 
 
+def gram_kernel(
+    slab_ref, idx_ref, coef_ref, out_ref,
+    buf, other_idx, later_ref, rows_ref, cols_ref, recv_sem, send_sem, idx_sem,
+):
+    group_cols = slab_ref.shape[2] // 2
+    x = lax.axis_index("lev")
+    h = lax.axis_index("hor")
+    z, y, c = h // 4, h // 2 % 2, h % 2
+
+    def along_z(k):
+        return (z // 2 + k // 2) % 2 * 2 + (z + k) % 2
+
+    def place(zz, yy, cc):
+        return zz * 4 + yy * 2 + cc
+
+    def piece(xx, hh, g):
+        return (xx * 16 + hh) * 2 + g
+
+    x_mate = (1 - x, h)
+    y_mate = (x, place(z, 1 - y, c))
+    core_mate = (x, place(z, y, 1 - c))
+    z_mates = [(x, place(along_z(k), y, c)) for k in (1, 2, 3)]
+
+    def send(p, target):
+        pltpu.make_async_remote_copy(
+            src_ref=buf.at[p], dst_ref=buf.at[p], send_sem=send_sem, recv_sem=recv_sem.at[p],
+            device_id=target, device_id_type=MESH,
+        ).start()
+
+    def arrive(p):
+        pltpu.make_async_copy(buf.at[p], buf.at[p], recv_sem.at[p]).wait()
+
+    barrier = pltpu.get_barrier_semaphore()
+    for mate in [x_mate, y_mate, core_mate] + z_mates:
+        pl.semaphore_signal(barrier, inc=1, device_id=mate, device_id_type=MESH)
+    pl.semaphore_wait(barrier, 6)
+
+    idx_copy = pltpu.make_async_remote_copy(
+        src_ref=idx_ref, dst_ref=other_idx, send_sem=idx_sem.at[0], recv_sem=idx_sem.at[1],
+        device_id=x_mate, device_id_type=MESH,
+    )
+    idx_copy.start()
+
+    def pick(g, idx_row):
+        step = 512
+        total = jnp.zeros((192, 128), jnp.float32)
+        for t in range(group_cols // step):
+            start = pl.multiple_of(g * group_cols + t * step, step)
+            v = slab_ref[:, :, pl.ds(start, step)].reshape(64, step)
+            hi = v.astype(jnp.bfloat16)
+            rest = v - hi.astype(jnp.float32)
+            mid = rest.astype(jnp.bfloat16)
+            low = (rest - mid.astype(jnp.float32)).astype(jnp.bfloat16)
+            parts = jnp.concatenate([hi, mid, low], axis=0)
+            lane = lax.broadcasted_iota(jnp.int32, (step, 128), 0) + t * step
+            hot = jnp.where(lane == idx_row, 1.0, 0.0).astype(jnp.bfloat16)
+            total += jnp.dot(parts, hot, preferred_element_type=jnp.float32)
+        p = piece(x, h, g)
+        buf[p] = total[0:64] + total[64:128] + total[128:192]
+        for mate in z_mates + [x_mate, y_mate, core_mate]:
+            send(p, mate)
+
+    pick(x, idx_ref[...])
+    idx_copy.wait_recv()
+    pick(1 - x, other_idx[...])
+
+    out_ref[...] = jnp.zeros_like(out_ref)
+
+    def forward_z(i, carry):
+        g = (x + i) % 2
+        p = piece(x, place(along_z(1 + i // 2), y, c), g)
+        arrive(p)
+        for mate in [x_mate, y_mate, core_mate]:
+            send(p, mate)
+        return carry
+
+    lax.fori_loop(0, 6, forward_z, 0)
+
+    first_row = 136 * h - 128
+    past_first = (h + 15) // 16
+    first_row = first_row * past_first
+    first_m = first_row // 32
+    row_start = pl.multiple_of(past_first * (128 + first_row - 32 * first_m), 8)
+
+    def add_block(hh):
+        for g in range(2):
+            lanes = slice(g * 128, g * 128 + 128)
+            below_p, above_p = piece(0, hh, g), piece(1, hh, g)
+            smooth = []
+            for f in range(4):
+                levels = slice(16 * f, 16 * f + 16)
+                v = jnp.concatenate([buf[below_p, levels, :], buf[above_p, levels, :]], axis=0)
+                smooth.append(
+                    coef_ref[0] * v
+                    + coef_ref[1] * pltpu.roll(v, 1, 0)
+                    + coef_ref[2] * pltpu.roll(v, 31, 0)
+                )
+            later_ref[g, 0:32, :] = smooth[2]
+            later_ref[g, 32:64, :] = smooth[3]
+            rows_ref[0:32, lanes] = smooth[2]
+            rows_ref[32:64, lanes] = smooth[3]
+            rows_ref[64:96, lanes] = smooth[0]
+            rows_ref[96:128, lanes] = smooth[1]
+            base = smooth[0]
+            for i in range(5):
+                m_row = later_ref[g, pl.ds(first_m + i, 1), :]
+                rows_ref[128 + 32 * i:160 + 32 * i, lanes] = m_row * base
+            for b in range(4, 34):
+                m_row = later_ref[g, pl.ds(b - 4 + 34 * x, 1), :]
+                cols_ref[32 * b:32 * b + 32, lanes] = (m_row * base).astype(jnp.bfloat16)
+
+            @pl.when(x == 0)
+            def _():
+                cols_ref[0:128, lanes] = rows_ref[0:128, lanes].astype(jnp.bfloat16)
+
+            @pl.when(x == 1)
+            def _():
+                s0 = rows_ref[64:96, lanes]
+                for b in range(4):
+                    cols_ref[32 * b:32 * b + 32, lanes] = (later_ref[g, 30 + b:31 + b, :] * s0).astype(jnp.bfloat16)
+
+        lhs = rows_ref[pl.ds(row_start, 136), :].astype(jnp.bfloat16)
+        out_ref[...] += lax.dot_general(
+            lhs, cols_ref[...], (((1,), (1,)), ((), ())), preferred_element_type=jnp.float32
+        )
+
+    def step(t, carry):
+        zz = along_z(t % 4)
+        far = t // 4
+        near = place(zz, y, c)
+        across = place(zz, 1 - y, c)
+
+        @pl.when(far == 0)
+        def _():
+            p = piece(1 - x, near, 1)
+            arrive(p)
+            send(p, y_mate)
+            send(p, core_mate)
+            p = piece(x, across, 0)
+            arrive(p)
+            send(p, x_mate)
+            send(p, core_mate)
+            for p in (piece(1 - x, near, 0), piece(x, across, 1)):
+                arrive(p)
+                send(p, core_mate)
+
+        @pl.when(far == 1)
+        def _():
+            for g in range(2):
+                p = piece(1 - x, across, g)
+                arrive(p)
+                send(p, core_mate)
+
+        yy = (y + far) % 2
+
+        def one(i, inner):
+            hh = place(zz, yy, (c + i) % 2)
+
+            @pl.when(i == 1)
+            def _():
+                for xx in range(2):
+                    for g in range(2):
+                        arrive(piece(xx, hh, g))
+
+            add_block(hh)
+            return inner
+
+        lax.fori_loop(0, 2, one, 0)
+        return carry
+
+    lax.fori_loop(0, 8, step, 0)
+    out_ref[...] = out_ref[...] * (1.0 / 4096)
+    sent = buf.at[pl.ds(0, 62)]
+    pltpu.make_async_copy(sent, sent, send_sem).wait()
+    idx_copy.wait_send()
+
+
+def on_slice(slab_fields, sample_index, thickness, level_cuts):
+    lower_weight, upper_weight = filter_weights(thickness, level_cuts)
+    denom = 2.0 * thickness + lower_weight + upper_weight
+    coef = jnp.stack([2.0 * thickness, lower_weight, upper_weight]) / denom
+    coef = jnp.broadcast_to(coef[:, :, None], (3, 32, 128))
+    vmem = pl.BlockSpec(memory_space=pltpu.VMEM)
+    return pl.pallas_call(
+        gram_kernel,
+        out_shape=jax.ShapeDtypeStruct((136, 1088), jnp.float32),
+        in_specs=[vmem] * 3,
+        out_specs=vmem,
+        scratch_shapes=[
+            pltpu.VMEM((64, 64, 128), jnp.float32),
+            pltpu.VMEM((1, 128), jnp.int32),
+            pltpu.VMEM((2, 64, 128), jnp.float32),
+            pltpu.VMEM((288, 256), jnp.float32),
+            pltpu.VMEM((1088, 256), jnp.bfloat16),
+            pltpu.SemaphoreType.DMA((64,)),
+            pltpu.SemaphoreType.DMA,
+            pltpu.SemaphoreType.DMA((2,)),
+        ],
+        compiler_params=pltpu.CompilerParams(
+            collective_id=0, has_side_effects=True, vmem_limit_bytes=32 * 1024 * 1024
+        ),
+    )(slab_fields, sample_index, coef)
+
+
 def solution(mesh):
     in_specs = (P(None, "lev", "hor"), P("hor", "lev"), P(), P())
     out_specs = P("hor", "lev")
+    small = mesh.shape["lev"] == 2 and mesh.shape["hor"] == 16
     return jax.shard_map(
-        on_device, mesh=mesh, in_specs=in_specs, out_specs=out_specs, check_vma=False
-    )
+        on_slice if small else general_plan,
+        mesh=mesh, in_specs=in_specs, out_specs=out_specs, check_vma=False,
+    )

time: 191 us -> 30.3 us (0.16)
  waiting for transfers between devices: 143 us -> 0 us
  Pallas kernels: 0 us -> 25.8 us
  between operations: 13.6 us -> 0.02 us
  local copies, waits for them, and re-layouts: 14.4 us -> 3.36 us
  matrix products: 6.84 us -> 0 us
  blocking collectives: 5.3 us -> 0 us
  starting transfers between devices: 3.38 us -> 0 us
  other arithmetic: 3.49 us -> 0.97 us
    unnamed x3 -> x0, waiting for transfers between devices: 117 us -> none
    pallas_call x0 -> x1, Pallas kernels: none -> 25.8 us  [on_slice(): pl.pallas_call(gram_kernel, out_shape=jax.ShapeDtypeStruct((136, 1088), j...]
    all_gather x1 -> x0, waiting for transfers between devices: 22.9 us -> none  [on_device(): block_features_bf = lax.all_gather(features_bf, 'lev', axis=1, tiled=True)]
    dot_general x1 -> x0, matrix products: 6.84 us -> none  [on_device(): lax.dot_general(block_features_bf, chosen_rows, (((1,), (1,)), ((), ())),...]
    unnamed x13 -> x7, local copies, waits for them, and re-layouts: 9.19 us -> 3.29 us
    all_gather x1 -> x0, blocking collectives: 5.3 us -> none  [on_device(): all_lists = lax.all_gather(sample_index, 'lev', axis=1, tiled=True)[0]]
    gather x1 -> x0, local copies, waits for them, and re-layouts: 4.42 us -> none  [on_device(): chosen = jnp.take(slab_fields, offsets, axis=2)]
    all_to_all x1 -> x0, waiting for transfers between devices: 3.88 us -> none  [on_device(): lax.all_to_all(chosen, 'lev', split_axis=2, concat_axis=1, tiled=True)]
  transfers between devices with their start and end apart: 3 -> 0, of which waited for: 3 -> 0; matrix products, arithmetic and copies ran while one was open for 0% -> 0% of each run, Pallas kernels for 0% -> 0%
where the time goes in v1:
time: 30.3 us; the launch traced here: 30.1 us
  Pallas kernels  25.8 us (85%)
  local copies, waits for them, and re-layouts  3.36 us (11%)
  other arithmetic  0.97 us (3%)
    pallas_call x1, Pallas kernels, on_slice(): pl.pallas_call(gram_kernel, out_shape=jax.ShapeDtypeStruct((136, 1088), j...  25.8 us
    unnamed x7, local copies, waits for them, and re-layouts  3.29 us
    sub x1, other arithmetic, filter_weights(): link = 1.0 - level_cuts.astype(jnp.float32)  0.8 us

profile of v1, /device:TPU:0, one launch (start us, length us, event | category | flops | bytes accessed | tf_op | source)
XLA Modules:
  0.0 30.1 jit_solution(4824809411013013894)
XLA Ops:
  0.0 0.8 %convert_subtract_fusion = (f32[31]{0:T(128)S(1)}, f32[1,31]{1,0:T(1,128)S(1)}, f32[31]{0:T(128)S(1)}, f32[1,31]{1,0:T(1,128)S(1)}, f32[1,31]{1,0:T(1,128)S(1)}, /*index=5*/f32[31]{0:T(128)S(1)}) fusion(s32[31]{0:T(128)} %param.7, f32[32]{0:T(128)} %param.6), kind=kLoop, calls=%fused_computation.15 | loop fusion | flops 62 | bytes 1116 | tf_op jit(solution)/shard_map/sub | solution.py:12
  0.8 0.0 copy-start.2
  0.8 0.7 %copy-done.2 = f32[32]{0:T(128)S(1)} copy-done((f32[32]{0:T(128)S(1)}, f32[32]{0:T(128)}, u32[]{:S(2)}) %copy-start.2) | copy-done | bytes 152
  1.5 0.1 fusion.1
  1.5 0.1 fusion.5
  1.6 0.0 copy-start.1
  1.6 0.1 broadcast_in_dim.2.coef_ref
  1.7 0.6 %copy-done.1 = s32[1,128]{1,0:T(1,128)S(1)} copy-done((s32[1,128]{1,0:T(1,128)S(1)}, s32[1,128]{1,0:T(1,128)}, u32[]{:S(2)}) %copy-start.1) | copy-done | bytes 536
  2.3 0.0 copy-start
  2.3 1.2 %copy-done = f32[4,16,4096]{2,1,0:T(8,128)S(1)} copy-done((f32[4,16,4096]{2,1,0:T(8,128)S(1)}, f32[4,16,4096]{2,1,0:T(8,128)}, u32[]{:S(2)}) %copy-start) | copy-done | bytes 1048600
  3.5 25.8 %shard_map.46 = f32[136,1088]{1,0:T(8,128)S(1)} custom-call(f32[4,16,4096]{2,1,0:T(8,128)S(1)} %copy-done, s32[1,128]{1,0:T(1,128)S(1)} %copy-done.1, f32[3,32,128]{2,1,0:T(8,128)S(1)} %broadcast_in_dim.2.coef_ref), custom_call_target="tpu_custom_call" | custom-call | tf_op jit(solution)/shard_map/pallas_call | solution.py:250
  29.3 0.8 %copy.6 = f32[136,1088]{1,0:T(8,128)} copy(f32[136,1088]{1,0:T(8,128)S(1)} %shard_map.46) | data formatting | bytes 1183744
  (1 shorter events, 0.0 us)
Async XLA Ops:
  0.8 0.7 %copy-start.2 = (f32[32]{0:T(128)S(1)}, f32[32]{0:T(128)}, u32[]{:S(2)}) copy-start(f32[32]{0:T(128)} %param.6) | copy-start | bytes 388
  1.6 0.7 %copy-start.1 = (s32[1,128]{1,0:T(1,128)S(1)}, s32[1,128]{1,0:T(1,128)}, u32[]{:S(2)}) copy-start(s32[1,128]{1,0:T(1,128)} %idx_ref.1) | copy-start | bytes 1540
  2.3 1.2 %copy-start = (f32[4,16,4096]{2,1,0:T(8,128)S(1)}, f32[4,16,4096]{2,1,0:T(8,128)}, u32[]{:S(2)}) copy-start(f32[4,16,4096]{2,1,0:T(8,128)} %slab_ref.1) | copy-start | bytes 3145732

commit v2 on v1

--- a/solution.py
+++ b/solution.py
@@ -65,8 +65,9 @@
 
 
 def gram_kernel(
-    slab_ref, idx_ref, coef_ref, out_ref,
-    buf, other_idx, later_ref, rows_ref, cols_ref, recv_sem, send_sem, idx_sem,
+    slab_hbm, idx_hbm, thick_hbm, cuts_hbm, out_ref,
+    slab_ref, idx_ref, thick_ref, cuts_ref, coef_ref, buf, other_idx,
+    later_ref, rows_ref, lhs_ref, cols_ref, recv_sem, send_sem, idx_sem, local_sem,
 ):
     group_cols = slab_ref.shape[2] // 2
     x = lax.axis_index("lev")
@@ -96,13 +97,28 @@
     def arrive(p):
         pltpu.make_async_copy(buf.at[p], buf.at[p], recv_sem.at[p]).wait()
 
+    def load_group(g, sem):
+        cols = pl.ds(pl.multiple_of(g * group_cols, group_cols), group_cols)
+        return pltpu.make_async_copy(slab_hbm.at[:, :, cols], slab_ref.at[:, :, cols], sem)
+
+    idx_load = pltpu.make_async_copy(idx_hbm, idx_ref, local_sem.at[0])
+    thick_load = pltpu.make_async_copy(thick_hbm, thick_ref, local_sem.at[1])
+    cuts_load = pltpu.make_async_copy(cuts_hbm, cuts_ref, local_sem.at[2])
+    own_load = load_group(x, local_sem.at[3])
+    other_load = load_group(1 - x, local_sem.at[4])
+    for load in (idx_load, own_load, thick_load, cuts_load, other_load):
+        load.start()
+
     barrier = pltpu.get_barrier_semaphore()
     for mate in [x_mate, y_mate, core_mate] + z_mates:
         pl.semaphore_signal(barrier, inc=1, device_id=mate, device_id_type=MESH)
+    out_ref[...] = jnp.zeros_like(out_ref)
+    lhs_ref[1] = jnp.zeros((136, 256), jnp.float32)
+    cols_ref[1] = jnp.zeros((1088, 256), jnp.bfloat16)
     pl.semaphore_wait(barrier, 6)
 
     idx_copy = pltpu.make_async_remote_copy(
-        src_ref=idx_ref, dst_ref=other_idx, send_sem=idx_sem.at[0], recv_sem=idx_sem.at[1],
+        src_ref=idx_hbm, dst_ref=other_idx, send_sem=idx_sem.at[0], recv_sem=idx_sem.at[1],
         device_id=x_mate, device_id_type=MESH,
     )
     idx_copy.start()
@@ -126,11 +142,32 @@
         for mate in z_mates + [x_mate, y_mate, core_mate]:
             send(p, mate)
 
+    idx_load.wait()
+    own_load.wait()
     pick(x, idx_ref[...])
+    other_load.wait()
     idx_copy.wait_recv()
     pick(1 - x, other_idx[...])
 
-    out_ref[...] = jnp.zeros_like(out_ref)
+    thick_load.wait()
+    cuts_load.wait()
+
+    def column(row, shift):
+        shape = (32, row.shape[1])
+        level = lax.broadcasted_iota(jnp.int32, shape, 0) + shift
+        hit = level == lax.broadcasted_iota(jnp.int32, shape, 1)
+        return jnp.sum(jnp.where(hit, row, 0.0), axis=1, keepdims=True)
+
+    thick = thick_ref[...]
+    link = 1.0 - cuts_ref[...].astype(jnp.float32)
+    weights = [
+        2.0 * column(thick, 0),
+        column(thick, -1) * column(link, -1),
+        column(thick, 1) * column(link, 0),
+    ]
+    denom = weights[0] + weights[1] + weights[2]
+    for i in range(3):
+        coef_ref[i] = jnp.broadcast_to(weights[i] / denom, (32, 128))
 
     def forward_z(i, carry):
         g = (x + i) % 2
@@ -142,13 +179,12 @@
 
     lax.fori_loop(0, 6, forward_z, 0)
 
-    first_row = 136 * h - 128
     past_first = (h + 15) // 16
-    first_row = first_row * past_first
+    first_row = (136 * h - 128) * past_first
     first_m = first_row // 32
     row_start = pl.multiple_of(past_first * (128 + first_row - 32 * first_m), 8)
 
-    def add_block(hh):
+    def features(hh, slot):
         for g in range(2):
             lanes = slice(g * 128, g * 128 + 128)
             below_p, above_p = piece(0, hh, g), piece(1, hh, g)
@@ -161,80 +197,81 @@
                     + coef_ref[1] * pltpu.roll(v, 1, 0)
                     + coef_ref[2] * pltpu.roll(v, 31, 0)
                 )
-            later_ref[g, 0:32, :] = smooth[2]
-            later_ref[g, 32:64, :] = smooth[3]
-            rows_ref[0:32, lanes] = smooth[2]
-            rows_ref[32:64, lanes] = smooth[3]
-            rows_ref[64:96, lanes] = smooth[0]
-            rows_ref[96:128, lanes] = smooth[1]
             base = smooth[0]
+            later_ref[slot, g, 0:32, :] = smooth[2]
+            later_ref[slot, g, 32:64, :] = smooth[3]
+            direct = [smooth[2], smooth[3], smooth[0], smooth[1]]
+            for b in range(4):
+                rows_ref[slot, 32 * b:32 * b + 32, lanes] = direct[b]
             for i in range(5):
-                m_row = later_ref[g, pl.ds(first_m + i, 1), :]
-                rows_ref[128 + 32 * i:160 + 32 * i, lanes] = m_row * base
-            for b in range(4, 34):
-                m_row = later_ref[g, pl.ds(b - 4 + 34 * x, 1), :]
-                cols_ref[32 * b:32 * b + 32, lanes] = (m_row * base).astype(jnp.bfloat16)
-
-            @pl.when(x == 0)
+                m_row = later_ref[slot, g, pl.ds(first_m + i, 1), :]
+                rows_ref[slot, 128 + 32 * i:160 + 32 * i, lanes] = m_row * base
+            for b in range(34):
+                if b < 4:
+                    m_row = later_ref[slot, g, 30 + b:31 + b, :]
+                    block = jnp.where(x == 0, direct[b], m_row * base)
+                else:
+                    m_row = later_ref[slot, g, pl.ds(b - 4 + 34 * x, 1), :]
+                    block = m_row * base
+                cols_ref[slot, 32 * b:32 * b + 32, lanes] = block.astype(jnp.bfloat16)
+        lhs_ref[slot] = rows_ref[slot, pl.ds(row_start, 136), :]
+
+    def add_product(slot):
+        out_ref[...] += lax.dot_general(
+            lhs_ref[slot].astype(jnp.bfloat16), cols_ref[slot],
+            (((1,), (1,)), ((), ())), preferred_element_type=jnp.float32,
+        )
+
+    def spread_near(k):
+        zz = along_z(k)
+        near, across = place(zz, y, c), place(zz, 1 - y, c)
+        p = piece(1 - x, near, 1)
+        arrive(p)
+        send(p, y_mate)
+        send(p, core_mate)
+        p = piece(x, across, 0)
+        arrive(p)
+        send(p, x_mate)
+        send(p, core_mate)
+        for p in (piece(1 - x, near, 0), piece(x, across, 1)):
+            arrive(p)
+            send(p, core_mate)
+
+    def spread_far(k):
+        for g in range(2):
+            p = piece(1 - x, place(along_z(k), 1 - y, c), g)
+            arrive(p)
+            send(p, core_mate)
+
+    def step(u, carry):
+        for half in range(2):
+            j = 2 * u + half
+
+            @pl.when(u < 2)
             def _():
-                cols_ref[0:128, lanes] = rows_ref[0:128, lanes].astype(jnp.bfloat16)
-
-            @pl.when(x == 1)
+                spread_near(j)
+
+            @pl.when((u - 1) // 2 == 1)
             def _():
-                s0 = rows_ref[64:96, lanes]
-                for b in range(4):
-                    cols_ref[32 * b:32 * b + 32, lanes] = (later_ref[g, 30 + b:31 + b, :] * s0).astype(jnp.bfloat16)
-
-        lhs = rows_ref[pl.ds(row_start, 136), :].astype(jnp.bfloat16)
-        out_ref[...] += lax.dot_general(
-            lhs, cols_ref[...], (((1,), (1,)), ((), ())), preferred_element_type=jnp.float32
-        )
-
-    def step(t, carry):
-        zz = along_z(t % 4)
-        far = t // 4
-        near = place(zz, y, c)
-        across = place(zz, 1 - y, c)
-
-        @pl.when(far == 0)
-        def _():
-            p = piece(1 - x, near, 1)
-            arrive(p)
-            send(p, y_mate)
-            send(p, core_mate)
-            p = piece(x, across, 0)
-            arrive(p)
-            send(p, x_mate)
-            send(p, core_mate)
-            for p in (piece(1 - x, near, 0), piece(x, across, 1)):
-                arrive(p)
-                send(p, core_mate)
-
-        @pl.when(far == 1)
-        def _():
-            for g in range(2):
-                p = piece(1 - x, across, g)
-                arrive(p)
-                send(p, core_mate)
-
-        yy = (y + far) % 2
-
-        def one(i, inner):
-            hh = place(zz, yy, (c + i) % 2)
-
-            @pl.when(i == 1)
+                spread_far(j - 6)
+
+            far = j // 8
+            mate = (1 - far) * (j // 4 % 2) + far * (j // 2 % 2)
+            k = (1 - far) * (j % 4) + far * (j % 8 // 4 * 2 + j % 2)
+            hh = place(along_z(k), (y + far) % 2, (c + mate) % 2)
+
+            @pl.when(mate == 1)
             def _():
                 for xx in range(2):
                     for g in range(2):
                         arrive(piece(xx, hh, g))
 
-            add_block(hh)
-            return inner
-
-        lax.fori_loop(0, 2, one, 0)
+            features(hh, half)
+            add_product(1 - half)
         return carry
 
     lax.fori_loop(0, 8, step, 0)
+    add_product(1)
     out_ref[...] = out_ref[...] * (1.0 / 4096)
     sent = buf.at[pl.ds(0, 62)]
     pltpu.make_async_copy(sent, sent, send_sem).wait()
@@ -242,30 +279,32 @@
 
 
 def on_slice(slab_fields, sample_index, thickness, level_cuts):
-    lower_weight, upper_weight = filter_weights(thickness, level_cuts)
-    denom = 2.0 * thickness + lower_weight + upper_weight
-    coef = jnp.stack([2.0 * thickness, lower_weight, upper_weight]) / denom
-    coef = jnp.broadcast_to(coef[:, :, None], (3, 32, 128))
-    vmem = pl.BlockSpec(memory_space=pltpu.VMEM)
     return pl.pallas_call(
         gram_kernel,
         out_shape=jax.ShapeDtypeStruct((136, 1088), jnp.float32),
-        in_specs=[vmem] * 3,
-        out_specs=vmem,
+        in_specs=[pl.BlockSpec(memory_space=pltpu.HBM)] * 4,
+        out_specs=pl.BlockSpec(memory_space=pltpu.VMEM),
         scratch_shapes=[
+            pltpu.VMEM(slab_fields.shape, jnp.float32),
+            pltpu.VMEM((1, 128), jnp.int32),
+            pltpu.VMEM((1, 32), jnp.float32),
+            pltpu.VMEM((1, 31), jnp.int32),
+            pltpu.VMEM((3, 32, 128), jnp.float32),
             pltpu.VMEM((64, 64, 128), jnp.float32),
             pltpu.VMEM((1, 128), jnp.int32),
-            pltpu.VMEM((2, 64, 128), jnp.float32),
-            pltpu.VMEM((288, 256), jnp.float32),
-            pltpu.VMEM((1088, 256), jnp.bfloat16),
+            pltpu.VMEM((2, 2, 64, 128), jnp.float32),
+            pltpu.VMEM((2, 288, 256), jnp.float32),
+            pltpu.VMEM((2, 136, 256), jnp.float32),
+            pltpu.VMEM((2, 1088, 256), jnp.bfloat16),
             pltpu.SemaphoreType.DMA((64,)),
             pltpu.SemaphoreType.DMA,
             pltpu.SemaphoreType.DMA((2,)),
+            pltpu.SemaphoreType.DMA((5,)),
         ],
         compiler_params=pltpu.CompilerParams(
-            collective_id=0, has_side_effects=True, vmem_limit_bytes=32 * 1024 * 1024
+            collective_id=0, has_side_effects=True, vmem_limit_bytes=60 * 1024 * 1024
         ),
-    )(slab_fields, sample_index, coef)
+    )(slab_fields, sample_index, thickness[None, :], level_cuts[None, :])
 
 
 def solution(mesh):

time: 30.3 us -> 27.6 us (0.911)
  local copies, waits for them, and re-layouts: 3.36 us -> 1.95 us
  other arithmetic: 0.97 us -> 0 us
    unnamed x7 -> x1, local copies, waits for them, and re-layouts: 3.29 us -> 1.95 us
    sub x1 -> x0, other arithmetic: 0.8 us -> none  [filter_weights(): link = 1.0 - level_cuts.astype(jnp.float32)]
where the time goes in v2:
time: 27.6 us; the launch traced here: 27.4 us
  Pallas kernels  25.5 us (92%)
  local copies, waits for them, and re-layouts  1.95 us (7%)
    pallas_call x1, Pallas kernels, on_slice(): pl.pallas_call(gram_kernel, out_shape=jax.ShapeDtypeStruct((136, 1088), j...  25.5 us
    unnamed x1, local copies, waits for them, and re-layouts  1.95 us

profile of v2, /device:TPU:0, one launch (start us, length us, event | category | flops | bytes accessed | tf_op | source)
XLA Modules:
  0.0 27.4 jit_solution(11180511646913487977)
XLA Ops:
  0.0 25.5 %shard_map.46 = f32[136,1088]{1,0:T(8,128)} custom-call(f32[4,16,4096]{2,1,0:T(8,128)} %slab_hbm.1, s32[1,128]{1,0:T(1,128)} %idx_hbm.1, f32[1,32]{1,0:T(1,128)} %bitcast.2, s32[1,31]{1,0:T(1,128)} %bitcast.3), custom_call_target="tpu_custom_call" | custom-call | tf_op jit(solution)/shard_map/pallas_call | solution.py:282
  25.5 1.9 %copy.6 = f32[136,1088]{1,0:T(8,128)} copy(f32[136,1088]{1,0:T(8,128)} %shard_map.46) | data formatting | bytes 1183744

commit v3 on v2

--- a/solution.py
+++ b/solution.py
@@ -67,7 +67,7 @@
 def gram_kernel(
     slab_hbm, idx_hbm, thick_hbm, cuts_hbm, out_ref,
     slab_ref, idx_ref, thick_ref, cuts_ref, coef_ref, buf, other_idx,
-    later_ref, rows_ref, lhs_ref, cols_ref, recv_sem, send_sem, idx_sem, local_sem,
+    later_ref, rows_ref, lhs_ref, cols_ref, acc_ref, recv_sem, send_sem, idx_sem, local_sem,
 ):
     group_cols = slab_ref.shape[2] // 2
     x = lax.axis_index("lev")
@@ -112,7 +112,7 @@
     barrier = pltpu.get_barrier_semaphore()
     for mate in [x_mate, y_mate, core_mate] + z_mates:
         pl.semaphore_signal(barrier, inc=1, device_id=mate, device_id_type=MESH)
-    out_ref[...] = jnp.zeros_like(out_ref)
+    acc_ref[...] = jnp.zeros_like(acc_ref)
     lhs_ref[1] = jnp.zeros((136, 256), jnp.float32)
     cols_ref[1] = jnp.zeros((1088, 256), jnp.bfloat16)
     pl.semaphore_wait(barrier, 6)
@@ -217,8 +217,8 @@
         lhs_ref[slot] = rows_ref[slot, pl.ds(row_start, 136), :]
 
     def add_product(slot):
-        out_ref[...] += lax.dot_general(
-            lhs_ref[slot].astype(jnp.bfloat16), cols_ref[slot],
+        acc_ref[...] += lax.dot_general(
+            cols_ref[slot], lhs_ref[slot].astype(jnp.bfloat16),
             (((1,), (1,)), ((), ())), preferred_element_type=jnp.float32,
         )
 
@@ -272,7 +272,7 @@
 
     lax.fori_loop(0, 8, step, 0)
     add_product(1)
-    out_ref[...] = out_ref[...] * (1.0 / 4096)
+    out_ref[...] = acc_ref[...].T * (1.0 / 4096)
     sent = buf.at[pl.ds(0, 62)]
     pltpu.make_async_copy(sent, sent, send_sem).wait()
     idx_copy.wait_send()
@@ -296,13 +296,14 @@
             pltpu.VMEM((2, 288, 256), jnp.float32),
             pltpu.VMEM((2, 136, 256), jnp.float32),
             pltpu.VMEM((2, 1088, 256), jnp.bfloat16),
+            pltpu.VMEM((1088, 136), jnp.float32),
             pltpu.SemaphoreType.DMA((64,)),
             pltpu.SemaphoreType.DMA,
             pltpu.SemaphoreType.DMA((2,)),
             pltpu.SemaphoreType.DMA((5,)),
         ],
         compiler_params=pltpu.CompilerParams(
-            collective_id=0, has_side_effects=True, vmem_limit_bytes=60 * 1024 * 1024
+            collective_id=0, has_side_effects=True, vmem_limit_bytes=53 * 1024 * 1024
         ),
     )(slab_fields, sample_index, thickness[None, :], level_cuts[None, :])
 

time: 27.6 us -> 28.2 us (1.022)
  Pallas kernels: 25.5 us -> 26.6 us
  local copies, waits for them, and re-layouts: 1.95 us -> 1.51 us
    pallas_call x1, Pallas kernels: 25.5 us -> 26.6 us  [on_slice(): pl.pallas_call(gram_kernel, out_shape=jax.ShapeDtypeStruct((136, 1088), j...]
    unnamed x1 -> x7, local copies, waits for them, and re-layouts: 1.95 us -> 1.51 us
where the time goes in v3:
time: 28.2 us; the launch traced here: 28.1 us
  Pallas kernels  26.6 us (94%)
  local copies, waits for them, and re-layouts  1.51 us (5%)
    pallas_call x1, Pallas kernels, on_slice(): pl.pallas_call(gram_kernel, out_shape=jax.ShapeDtypeStruct((136, 1088), j...  26.6 us
    unnamed x7, local copies, waits for them, and re-layouts  1.51 us

profile of v3, /device:TPU:0, one launch (start us, length us, event | category | flops | bytes accessed | tf_op | source)
XLA Modules:
  0.0 28.1 jit_solution(17666558521772474486)
XLA Ops:
  0.0 0.0 copy-start
  0.0 0.0 copy-start.1
  0.0 0.0 copy-start.2
  0.0 0.6 %copy-done = s32[1,128]{1,0:T(1,128)S(1)} copy-done((s32[1,128]{1,0:T(1,128)S(1)}, s32[1,128]{1,0:T(1,128)}, u32[]{:S(2)}) %copy-start) | copy-done | bytes 536
  0.7 0.0 copy-done.1
  0.7 0.0 copy-done.2
  0.7 26.6 %shard_map.46 = f32[136,1088]{1,0:T(8,128)S(1)} custom-call(f32[4,16,4096]{2,1,0:T(8,128)} %slab_hbm.1, s32[1,128]{1,0:T(1,128)S(1)} %copy-done, f32[1,32]{1,0:T(1,128)S(1)} %bitcast.2, s32[1,31]{1,0:T(1,128)S(1)} %bitcast.3), custom_call_target="tpu_custom_call" | custom-call | tf_op jit(solution)/shard_map/pallas_call | solution.py:282
  27.3 0.8 %copy.6 = f32[136,1088]{1,0:T(8,128)} copy(f32[136,1088]{1,0:T(8,128)S(1)} %shard_map.46) | data formatting | bytes 1183744
Async XLA Ops:
  0.0 0.7 %copy-start = (s32[1,128]{1,0:T(1,128)S(1)}, s32[1,128]{1,0:T(1,128)}, u32[]{:S(2)}) copy-start(s32[1,128]{1,0:T(1,128)} %idx_hbm.1) | copy-start | bytes 1540
  0.0 0.7 %copy-start.1 = (f32[32]{0:T(128)S(1)}, f32[32]{0:T(128)}, u32[]{:S(2)}) copy-start(f32[32]{0:T(128)} %param.6) | copy-start | bytes 388
  0.0 0.7 %copy-start.2 = (s32[31]{0:T(128)S(1)}, s32[31]{0:T(128)}, u32[]{:S(2)}) copy-start(s32[31]{0:T(128)} %param.7) | copy-start | bytes 376

commit v4 on v2

--- a/solution.py
+++ b/solution.py
@@ -67,7 +67,7 @@
 def gram_kernel(
     slab_hbm, idx_hbm, thick_hbm, cuts_hbm, out_ref,
     slab_ref, idx_ref, thick_ref, cuts_ref, coef_ref, buf, other_idx,
-    later_ref, rows_ref, lhs_ref, cols_ref, recv_sem, send_sem, idx_sem, local_sem,
+    rows_ref, cols_ref, recv_sem, send_sem, idx_sem, local_sem,
 ):
     group_cols = slab_ref.shape[2] // 2
     x = lax.axis_index("lev")
@@ -113,8 +113,8 @@
     for mate in [x_mate, y_mate, core_mate] + z_mates:
         pl.semaphore_signal(barrier, inc=1, device_id=mate, device_id_type=MESH)
     out_ref[...] = jnp.zeros_like(out_ref)
-    lhs_ref[1] = jnp.zeros((136, 256), jnp.float32)
-    cols_ref[1] = jnp.zeros((1088, 256), jnp.bfloat16)
+    rows_ref[1] = jnp.zeros((4, 288, 128), jnp.float32)
+    cols_ref[1] = jnp.zeros((1088, 512), jnp.bfloat16)
     pl.semaphore_wait(barrier, 6)
 
     idx_copy = pltpu.make_async_remote_copy(
@@ -139,7 +139,7 @@
             total += jnp.dot(parts, hot, preferred_element_type=jnp.float32)
         p = piece(x, h, g)
         buf[p] = total[0:64] + total[64:128] + total[128:192]
-        for mate in z_mates + [x_mate, y_mate, core_mate]:
+        for mate in [x_mate, y_mate] + z_mates + [core_mate]:
             send(p, mate)
 
     idx_load.wait()
@@ -184,9 +184,10 @@
     first_m = first_row // 32
     row_start = pl.multiple_of(past_first * (128 + first_row - 32 * first_m), 8)
 
-    def features(hh, slot):
+    def features(hh, slot, half):
         for g in range(2):
-            lanes = slice(g * 128, g * 128 + 128)
+            lanes = slice(half * 256 + g * 128, half * 256 + g * 128 + 128)
+            q = half * 2 + g
             below_p, above_p = piece(0, hh, g), piece(1, hh, g)
             smooth = []
             for f in range(4):
@@ -198,27 +199,26 @@
                     + coef_ref[2] * pltpu.roll(v, 31, 0)
                 )
             base = smooth[0]
-            later_ref[slot, g, 0:32, :] = smooth[2]
-            later_ref[slot, g, 32:64, :] = smooth[3]
             direct = [smooth[2], smooth[3], smooth[0], smooth[1]]
             for b in range(4):
-                rows_ref[slot, 32 * b:32 * b + 32, lanes] = direct[b]
+                rows_ref[slot, q, 32 * b:32 * b + 32, :] = direct[b]
             for i in range(5):
-                m_row = later_ref[slot, g, pl.ds(first_m + i, 1), :]
-                rows_ref[slot, 128 + 32 * i:160 + 32 * i, lanes] = m_row * base
+                m_row = rows_ref[slot, q, pl.ds(first_m + i, 1), :]
+                rows_ref[slot, q, 128 + 32 * i:160 + 32 * i, :] = m_row * base
+            chosen = jnp.where(x == 0, smooth[2], pltpu.roll(smooth[3], 30, 0))
             for b in range(34):
-                if b < 4:
-                    m_row = later_ref[slot, g, 30 + b:31 + b, :]
-                    block = jnp.where(x == 0, direct[b], m_row * base)
+                if b < 2:
+                    block = jnp.where(x == 0, direct[b], smooth[2][30 + b:31 + b] * base)
+                elif b < 4:
+                    block = jnp.where(x == 0, direct[b], smooth[3][b - 2:b - 1] * base)
                 else:
-                    m_row = later_ref[slot, g, pl.ds(b - 4 + 34 * x, 1), :]
-                    block = m_row * base
+                    block = chosen[b - 4:b - 3] * base
                 cols_ref[slot, 32 * b:32 * b + 32, lanes] = block.astype(jnp.bfloat16)
-        lhs_ref[slot] = rows_ref[slot, pl.ds(row_start, 136), :]
 
     def add_product(slot):
+        own = [rows_ref[slot, q, pl.ds(row_start, 136), :] for q in range(4)]
         out_ref[...] += lax.dot_general(
-            lhs_ref[slot].astype(jnp.bfloat16), cols_ref[slot],
+            jnp.concatenate(own, axis=1).astype(jnp.bfloat16), cols_ref[slot],
             (((1,), (1,)), ((), ())), preferred_element_type=jnp.float32,
         )
 
@@ -244,14 +244,14 @@
             send(p, core_mate)
 
     def step(u, carry):
-        for half in range(2):
-            j = 2 * u + half
-
-            @pl.when(u < 2)
+        for part in range(4):
+            j = 4 * u + part
+
+            @pl.when(u == 0)
             def _():
                 spread_near(j)
 
-            @pl.when((u - 1) // 2 == 1)
+            @pl.when((j + 2) // 4 == 2)
             def _():
                 spread_far(j - 6)
 
@@ -266,11 +266,12 @@
                     for g in range(2):
                         arrive(piece(xx, hh, g))
 
-            features(hh, half)
-            add_product(1 - half)
+            features(hh, part // 2, part % 2)
+            if part % 2 == 1:
+                add_product(1 - part // 2)
         return carry
 
-    lax.fori_loop(0, 8, step, 0)
+    lax.fori_loop(0, 4, step, 0)
     add_product(1)
     out_ref[...] = out_ref[...] * (1.0 / 4096)
     sent = buf.at[pl.ds(0, 62)]
@@ -292,17 +293,15 @@
             pltpu.VMEM((3, 32, 128), jnp.float32),
             pltpu.VMEM((64, 64, 128), jnp.float32),
             pltpu.VMEM((1, 128), jnp.int32),
-            pltpu.VMEM((2, 2, 64, 128), jnp.float32),
-            pltpu.VMEM((2, 288, 256), jnp.float32),
-            pltpu.VMEM((2, 136, 256), jnp.float32),
-            pltpu.VMEM((2, 1088, 256), jnp.bfloat16),
+            pltpu.VMEM((2, 4, 288, 128), jnp.float32),
+            pltpu.VMEM((2, 1088, 512), jnp.bfloat16),
             pltpu.SemaphoreType.DMA((64,)),
             pltpu.SemaphoreType.DMA,
             pltpu.SemaphoreType.DMA((2,)),
             pltpu.SemaphoreType.DMA((5,)),
         ],
         compiler_params=pltpu.CompilerParams(
-            collective_id=0, has_side_effects=True, vmem_limit_bytes=60 * 1024 * 1024
+            collective_id=0, has_side_effects=True, vmem_limit_bytes=53 * 1024 * 1024
         ),
     )(slab_fields, sample_index, thickness[None, :], level_cuts[None, :])
 

time: 27.6 us -> 26.7 us (0.967)
  Pallas kernels: 25.5 us -> 25 us
  local copies, waits for them, and re-layouts: 1.95 us -> 1.51 us
    pallas_call x1, Pallas kernels: 25.5 us -> 25 us  [on_slice(): pl.pallas_call(gram_kernel, out_shape=jax.ShapeDtypeStruct((136, 1088), j...]
    unnamed x1 -> x7, local copies, waits for them, and re-layouts: 1.95 us -> 1.51 us
where the time goes in v4:
time: 26.7 us; the launch traced here: 26.6 us
  Pallas kernels  25 us (94%)
  local copies, waits for them, and re-layouts  1.51 us (6%)
    pallas_call x1, Pallas kernels, on_slice(): pl.pallas_call(gram_kernel, out_shape=jax.ShapeDtypeStruct((136, 1088), j...  25 us
    unnamed x7, local copies, waits for them, and re-layouts  1.51 us

profile of v4, /device:TPU:0, one launch (start us, length us, event | category | flops | bytes accessed | tf_op | source)
XLA Modules:
  0.0 26.6 jit_solution(1323471287378857193)
XLA Ops:
  0.0 0.0 copy-start
  0.0 0.0 copy-start.1
  0.0 0.0 copy-start.2
  0.0 0.6 %copy-done = s32[1,128]{1,0:T(1,128)S(1)} copy-done((s32[1,128]{1,0:T(1,128)S(1)}, s32[1,128]{1,0:T(1,128)}, u32[]{:S(2)}) %copy-start) | copy-done | bytes 536
  0.7 0.0 copy-done.1
  0.7 0.0 copy-done.2
  0.7 25.0 %shard_map.46 = f32[136,1088]{1,0:T(8,128)S(1)} custom-call(f32[4,16,4096]{2,1,0:T(8,128)} %slab_hbm.1, s32[1,128]{1,0:T(1,128)S(1)} %copy-done, f32[1,32]{1,0:T(1,128)S(1)} %bitcast.2, s32[1,31]{1,0:T(1,128)S(1)} %bitcast.3), custom_call_target="tpu_custom_call" | custom-call | tf_op jit(solution)/shard_map/pallas_call | solution.py:283
  25.7 0.8 %copy.6 = f32[136,1088]{1,0:T(8,128)} copy(f32[136,1088]{1,0:T(8,128)S(1)} %shard_map.46) | data formatting | bytes 1183744
Async XLA Ops:
  0.0 0.7 %copy-start = (s32[1,128]{1,0:T(1,128)S(1)}, s32[1,128]{1,0:T(1,128)}, u32[]{:S(2)}) copy-start(s32[1,128]{1,0:T(1,128)} %idx_hbm.1) | copy-start | bytes 1540
  0.0 0.7 %copy-start.1 = (f32[32]{0:T(128)S(1)}, f32[32]{0:T(128)}, u32[]{:S(2)}) copy-start(f32[32]{0:T(128)} %param.6) | copy-start | bytes 388
  0.0 0.7 %copy-start.2 = (s32[31]{0:T(128)S(1)}, s32[31]{0:T(128)}, u32[]{:S(2)}) copy-start(s32[31]{0:T(128)} %param.7) | copy-start | bytes 376

commit v5 on v4

--- a/solution.py
+++ b/solution.py
@@ -75,7 +75,9 @@
     z, y, c = h // 4, h // 2 % 2, h % 2
 
     def along_z(k):
-        return (z // 2 + k // 2) % 2 * 2 + (z + k) % 2
+        table = 228 + 145 * 256 + 122 * 256**2 + 15 * 256**3
+        unit = (1 + 255 * (k % 2)) * (1 + 65535 * (k // 2)) * (1 + 3 * (z % 2)) * (1 + 15 * (z // 2))
+        return table // unit % 4
 
     def place(zz, yy, cc):
         return zz * 4 + yy * 2 + cc
@@ -86,11 +88,12 @@
     x_mate = (1 - x, h)
     y_mate = (x, place(z, 1 - y, c))
     core_mate = (x, place(z, y, 1 - c))
-    z_mates = [(x, place(along_z(k), y, c)) for k in (1, 2, 3)]
-
-    def send(p, target):
+    up_mate = (x, place((z + 1) % 4, y, c))
+    down_mate = (x, place((z + 3) % 4, y, c))
+
+    def send(p, target, sem=0):
         pltpu.make_async_remote_copy(
-            src_ref=buf.at[p], dst_ref=buf.at[p], send_sem=send_sem, recv_sem=recv_sem.at[p],
+            src_ref=buf.at[p], dst_ref=buf.at[p], send_sem=send_sem.at[sem], recv_sem=recv_sem.at[p],
             device_id=target, device_id_type=MESH,
         ).start()
 
@@ -110,12 +113,21 @@
         load.start()
 
     barrier = pltpu.get_barrier_semaphore()
-    for mate in [x_mate, y_mate, core_mate] + z_mates:
+    for mate in [x_mate, y_mate, core_mate]:
         pl.semaphore_signal(barrier, inc=1, device_id=mate, device_id_type=MESH)
+
+    @pl.when(z < 3)
+    def _():
+        pl.semaphore_signal(barrier, inc=1, device_id=up_mate, device_id_type=MESH)
+
+    @pl.when(z > 0)
+    def _():
+        pl.semaphore_signal(barrier, inc=1, device_id=down_mate, device_id_type=MESH)
+
     out_ref[...] = jnp.zeros_like(out_ref)
     rows_ref[1] = jnp.zeros((4, 288, 128), jnp.float32)
     cols_ref[1] = jnp.zeros((1088, 512), jnp.bfloat16)
-    pl.semaphore_wait(barrier, 6)
+    pl.semaphore_wait(barrier, 5 - z // 3 - (3 - z) // 3)
 
     idx_copy = pltpu.make_async_remote_copy(
         src_ref=idx_hbm, dst_ref=other_idx, send_sem=idx_sem.at[0], recv_sem=idx_sem.at[1],
@@ -139,7 +151,16 @@
             total += jnp.dot(parts, hot, preferred_element_type=jnp.float32)
         p = piece(x, h, g)
         buf[p] = total[0:64] + total[64:128] + total[128:192]
-        for mate in [x_mate, y_mate] + z_mates + [core_mate]:
+
+        @pl.when(z < 3)
+        def _():
+            send(p, up_mate, 1)
+
+        @pl.when(z > 0)
+        def _():
+            send(p, down_mate, 1)
+
+        for mate in [x_mate, y_mate, core_mate]:
             send(p, mate)
 
     idx_load.wait()
@@ -169,15 +190,22 @@
     for i in range(3):
         coef_ref[i] = jnp.broadcast_to(weights[i] / denom, (32, 128))
 
-    def forward_z(i, carry):
-        g = (x + i) % 2
-        p = piece(x, place(along_z(1 + i // 2), y, c), g)
-        arrive(p)
-        for mate in [x_mate, y_mate, core_mate]:
-            send(p, mate)
-        return carry
-
-    lax.fori_loop(0, 6, forward_z, 0)
+    def spread_z(k):
+        zz = along_z(k)
+        for i in range(2):
+            p = piece(x, place(zz, y, c), (x + i) % 2)
+            arrive(p)
+
+            @pl.when((zz < z) & (z < 3))
+            def _():
+                send(p, up_mate, 1)
+
+            @pl.when((zz > z) & (z > 0))
+            def _():
+                send(p, down_mate, 1)
+
+            for mate in [x_mate, y_mate, core_mate]:
+                send(p, mate)
 
     past_first = (h + 15) // 16
     first_row = (136 * h - 128) * past_first
@@ -247,13 +275,21 @@
         for part in range(4):
             j = 4 * u + part
 
-            @pl.when(u == 0)
-            def _():
-                spread_near(j)
-
-            @pl.when((j + 2) // 4 == 2)
-            def _():
-                spread_far(j - 6)
+            if part == 1:
+                @pl.when(j == 1)
+                def _():
+                    spread_z(3)
+                    spread_near(2)
+
+            if part == 2:
+                @pl.when(j == 2)
+                def _():
+                    spread_near(3)
+
+            if part % 2 == 1:
+                @pl.when((j >= 3) & (j <= 9))
+                def _():
+                    spread_far((j - 3) // 2)
 
             far = j // 8
             mate = (1 - far) * (j // 4 % 2) + far * (j // 2 % 2)
@@ -271,11 +307,29 @@
                 add_product(1 - part // 2)
         return carry
 
+    spread_z(1)
+    spread_near(0)
+    spread_z(2)
+    spread_near(1)
     lax.fori_loop(0, 4, step, 0)
     add_product(1)
     out_ref[...] = out_ref[...] * (1.0 / 4096)
-    sent = buf.at[pl.ds(0, 62)]
-    pltpu.make_async_copy(sent, sent, send_sem).wait()
+
+    def all_sent(count, sem):
+        sent = buf.at[pl.ds(0, count)]
+        pltpu.make_async_copy(sent, sent, send_sem.at[sem]).wait()
+
+    all_sent(56, 0)
+    middle = (z + 1) // 2 % 2
+
+    @pl.when(middle == 1)
+    def _():
+        all_sent(10, 1)
+
+    @pl.when(middle == 0)
+    def _():
+        all_sent(2, 1)
+
     idx_copy.wait_send()
 
 
@@ -296,7 +350,7 @@
             pltpu.VMEM((2, 4, 288, 128), jnp.float32),
             pltpu.VMEM((2, 1088, 512), jnp.bfloat16),
             pltpu.SemaphoreType.DMA((64,)),
-            pltpu.SemaphoreType.DMA,
+            pltpu.SemaphoreType.DMA((2,)),
             pltpu.SemaphoreType.DMA((2,)),
             pltpu.SemaphoreType.DMA((5,)),
         ],

time: 26.7 us -> 29.5 us (1.10)
  Pallas kernels: 25 us -> 27.8 us
    pallas_call x1, Pallas kernels: 25 us -> 27.8 us  [on_slice(): pl.pallas_call(gram_kernel, out_shape=jax.ShapeDtypeStruct((136, 1088), j...]
where the time goes in v5:
time: 29.5 us; the launch traced here: 29.3 us
  Pallas kernels  27.8 us (94%)
  local copies, waits for them, and re-layouts  1.51 us (5%)
    pallas_call x1, Pallas kernels, on_slice(): pl.pallas_call(gram_kernel, out_shape=jax.ShapeDtypeStruct((136, 1088), j...  27.8 us
    unnamed x7, local copies, waits for them, and re-layouts  1.51 us

profile of v5, /device:TPU:0, one launch (start us, length us, event | category | flops | bytes accessed | tf_op | source)
XLA Modules:
  0.0 29.3 jit_solution(10012973653018179116)
XLA Ops:
  0.0 0.0 copy-start
  0.0 0.0 copy-start.1
  0.0 0.0 copy-start.2
  0.0 0.6 %copy-done = s32[1,128]{1,0:T(1,128)S(1)} copy-done((s32[1,128]{1,0:T(1,128)S(1)}, s32[1,128]{1,0:T(1,128)}, u32[]{:S(2)}) %copy-start) | copy-done | bytes 536
  0.7 0.0 copy-done.1
  0.7 0.0 copy-done.2
  0.7 27.8 %shard_map.46 = f32[136,1088]{1,0:T(8,128)S(1)} custom-call(f32[4,16,4096]{2,1,0:T(8,128)} %slab_hbm.1, s32[1,128]{1,0:T(1,128)S(1)} %copy-done, f32[1,32]{1,0:T(1,128)S(1)} %bitcast.2, s32[1,31]{1,0:T(1,128)S(1)} %bitcast.3), custom_call_target="tpu_custom_call" | custom-call | tf_op jit(solution)/shard_map/pallas_call | solution.py:337
  28.5 0.8 %copy.6 = f32[136,1088]{1,0:T(8,128)} copy(f32[136,1088]{1,0:T(8,128)S(1)} %shard_map.46) | data formatting | bytes 1183744
Async XLA Ops:
  0.0 0.7 %copy-start = (s32[1,128]{1,0:T(1,128)S(1)}, s32[1,128]{1,0:T(1,128)}, u32[]{:S(2)}) copy-start(s32[1,128]{1,0:T(1,128)} %idx_hbm.1) | copy-start | bytes 1540
  0.0 0.7 %copy-start.1 = (f32[32]{0:T(128)S(1)}, f32[32]{0:T(128)}, u32[]{:S(2)}) copy-start(f32[32]{0:T(128)} %param.6) | copy-start | bytes 388
  0.0 0.7 %copy-start.2 = (s32[31]{0:T(128)S(1)}, s32[31]{0:T(128)}, u32[]{:S(2)}) copy-start(s32[31]{0:T(128)} %param.7) | copy-start | bytes 376

commit v6 on v4

--- a/solution.py
+++ b/solution.py
@@ -75,22 +75,25 @@
     z, y, c = h // 4, h // 2 % 2, h % 2
 
     def along_z(k):
-        return (z // 2 + k // 2) % 2 * 2 + (z + k) % 2
+        table = 228 + 145 * 256 + 122 * 256**2 + 15 * 256**3
+        unit = (1 + 255 * (k % 2)) * (1 + 65535 * (k // 2)) * (1 + 3 * (z % 2)) * (1 + 15 * (z // 2))
+        return table // unit % 4
 
     def place(zz, yy, cc):
         return zz * 4 + yy * 2 + cc
 
-    def piece(xx, hh, g):
-        return (xx * 16 + hh) * 2 + g
+    def pair(xx, hh):
+        return xx * 16 + hh
 
     x_mate = (1 - x, h)
     y_mate = (x, place(z, 1 - y, c))
     core_mate = (x, place(z, y, 1 - c))
     z_mates = [(x, place(along_z(k), y, c)) for k in (1, 2, 3)]
 
-    def send(p, target):
+    def send(p, target, g=None):
+        part = buf.at[p] if g is None else buf.at[p, g]
         pltpu.make_async_remote_copy(
-            src_ref=buf.at[p], dst_ref=buf.at[p], send_sem=send_sem, recv_sem=recv_sem.at[p],
+            src_ref=part, dst_ref=part, send_sem=send_sem, recv_sem=recv_sem.at[p],
             device_id=target, device_id_type=MESH,
         ).start()
 
@@ -137,10 +140,10 @@
             lane = lax.broadcasted_iota(jnp.int32, (step, 128), 0) + t * step
             hot = jnp.where(lane == idx_row, 1.0, 0.0).astype(jnp.bfloat16)
             total += jnp.dot(parts, hot, preferred_element_type=jnp.float32)
-        p = piece(x, h, g)
-        buf[p] = total[0:64] + total[64:128] + total[128:192]
-        for mate in [x_mate, y_mate] + z_mates + [core_mate]:
-            send(p, mate)
+        p = pair(x, h)
+        buf[p, g] = total[0:64] + total[64:128] + total[128:192]
+        for mate in z_mates + [x_mate, y_mate, core_mate]:
+            send(p, mate, g)
 
     idx_load.wait()
     own_load.wait()
@@ -169,15 +172,11 @@
     for i in range(3):
         coef_ref[i] = jnp.broadcast_to(weights[i] / denom, (32, 128))
 
-    def forward_z(i, carry):
-        g = (x + i) % 2
-        p = piece(x, place(along_z(1 + i // 2), y, c), g)
+    def spread_z(k):
+        p = pair(x, place(along_z(k), y, c))
         arrive(p)
         for mate in [x_mate, y_mate, core_mate]:
             send(p, mate)
-        return carry
-
-    lax.fori_loop(0, 6, forward_z, 0)
 
     past_first = (h + 15) // 16
     first_row = (136 * h - 128) * past_first
@@ -188,11 +187,11 @@
         for g in range(2):
             lanes = slice(half * 256 + g * 128, half * 256 + g * 128 + 128)
             q = half * 2 + g
-            below_p, above_p = piece(0, hh, g), piece(1, hh, g)
+            below_p, above_p = pair(0, hh), pair(1, hh)
             smooth = []
             for f in range(4):
                 levels = slice(16 * f, 16 * f + 16)
-                v = jnp.concatenate([buf[below_p, levels, :], buf[above_p, levels, :]], axis=0)
+                v = jnp.concatenate([buf[below_p, g, levels, :], buf[above_p, g, levels, :]], axis=0)
                 smooth.append(
                     coef_ref[0] * v
                     + coef_ref[1] * pltpu.roll(v, 1, 0)
@@ -224,36 +223,33 @@
 
     def spread_near(k):
         zz = along_z(k)
-        near, across = place(zz, y, c), place(zz, 1 - y, c)
-        p = piece(1 - x, near, 1)
+        p = pair(1 - x, place(zz, y, c))
         arrive(p)
-        send(p, y_mate)
+        send(p, y_mate, 1)
         send(p, core_mate)
-        p = piece(x, across, 0)
+        p = pair(x, place(zz, 1 - y, c))
         arrive(p)
-        send(p, x_mate)
+        send(p, x_mate, 0)
         send(p, core_mate)
-        for p in (piece(1 - x, near, 0), piece(x, across, 1)):
-            arrive(p)
-            send(p, core_mate)
 
     def spread_far(k):
-        for g in range(2):
-            p = piece(1 - x, place(along_z(k), 1 - y, c), g)
-            arrive(p)
-            send(p, core_mate)
+        p = pair(1 - x, place(along_z(k), 1 - y, c))
+        arrive(p)
+        send(p, core_mate)
 
     def step(u, carry):
         for part in range(4):
             j = 4 * u + part
 
-            @pl.when(u == 0)
-            def _():
-                spread_near(j)
-
-            @pl.when((j + 2) // 4 == 2)
-            def _():
-                spread_far(j - 6)
+            if part < 2:
+                @pl.when(u == 0)
+                def _():
+                    spread_near(2 + part)
+
+            if part % 2 == 1:
+                @pl.when((j >= 3) & (j <= 9))
+                def _():
+                    spread_far((j - 3) // 2)
 
             far = j // 8
             mate = (1 - far) * (j // 4 % 2) + far * (j // 2 % 2)
@@ -263,18 +259,22 @@
             @pl.when(mate == 1)
             def _():
                 for xx in range(2):
-                    for g in range(2):
-                        arrive(piece(xx, hh, g))
+                    arrive(pair(xx, hh))
 
             features(hh, part // 2, part % 2)
             if part % 2 == 1:
                 add_product(1 - part // 2)
         return carry
 
+    spread_z(1)
+    spread_near(0)
+    spread_z(2)
+    spread_near(1)
+    spread_z(3)
     lax.fori_loop(0, 4, step, 0)
     add_product(1)
     out_ref[...] = out_ref[...] * (1.0 / 4096)
-    sent = buf.at[pl.ds(0, 62)]
+    sent = buf.at[pl.ds(0, 31)]
     pltpu.make_async_copy(sent, sent, send_sem).wait()
     idx_copy.wait_send()
 
@@ -291,11 +291,11 @@
             pltpu.VMEM((1, 32), jnp.float32),
             pltpu.VMEM((1, 31), jnp.int32),
             pltpu.VMEM((3, 32, 128), jnp.float32),
-            pltpu.VMEM((64, 64, 128), jnp.float32),
+            pltpu.VMEM((32, 2, 64, 128), jnp.float32),
             pltpu.VMEM((1, 128), jnp.int32),
             pltpu.VMEM((2, 4, 288, 128), jnp.float32),
             pltpu.VMEM((2, 1088, 512), jnp.bfloat16),
-            pltpu.SemaphoreType.DMA((64,)),
+            pltpu.SemaphoreType.DMA((32,)),
             pltpu.SemaphoreType.DMA,
             pltpu.SemaphoreType.DMA((2,)),
             pltpu.SemaphoreType.DMA((5,)),

time: 26.7 us -> 29 us (1.086)
  Pallas kernels: 25 us -> 27.4 us
    pallas_call x1, Pallas kernels: 25 us -> 27.4 us  [on_slice(): pl.pallas_call(gram_kernel, out_shape=jax.ShapeDtypeStruct((136, 1088), j...]
where the time goes in v6:
time: 29 us; the launch traced here: 28.9 us
  Pallas kernels  27.4 us (94%)
  local copies, waits for them, and re-layouts  1.51 us (5%)
    pallas_call x1, Pallas kernels, on_slice(): pl.pallas_call(gram_kernel, out_shape=jax.ShapeDtypeStruct((136, 1088), j...  27.4 us
    unnamed x7, local copies, waits for them, and re-layouts  1.51 us

profile of v6, /device:TPU:0, one launch (start us, length us, event | category | flops | bytes accessed | tf_op | source)
XLA Modules:
  0.0 28.9 jit_solution(17698952965148834288)
XLA Ops:
  0.0 0.0 copy-start
  0.0 0.0 copy-start.1
  0.0 0.0 copy-start.2
  0.0 0.6 %copy-done = s32[1,128]{1,0:T(1,128)S(1)} copy-done((s32[1,128]{1,0:T(1,128)S(1)}, s32[1,128]{1,0:T(1,128)}, u32[]{:S(2)}) %copy-start) | copy-done | bytes 536
  0.7 0.0 copy-done.1
  0.7 0.0 copy-done.2
  0.7 27.4 %shard_map.46 = f32[136,1088]{1,0:T(8,128)S(1)} custom-call(f32[4,16,4096]{2,1,0:T(8,128)} %slab_hbm.1, s32[1,128]{1,0:T(1,128)S(1)} %copy-done, f32[1,32]{1,0:T(1,128)S(1)} %bitcast.2, s32[1,31]{1,0:T(1,128)S(1)} %bitcast.3), custom_call_target="tpu_custom_call" | custom-call | tf_op jit(solution)/shard_map/pallas_call | solution.py:283
  28.0 0.8 %copy.6 = f32[136,1088]{1,0:T(8,128)} copy(f32[136,1088]{1,0:T(8,128)S(1)} %shard_map.46) | data formatting | bytes 1183744
Async XLA Ops:
  0.0 0.7 %copy-start = (s32[1,128]{1,0:T(1,128)S(1)}, s32[1,128]{1,0:T(1,128)}, u32[]{:S(2)}) copy-start(s32[1,128]{1,0:T(1,128)} %idx_hbm.1) | copy-start | bytes 1540
  0.0 0.7 %copy-start.1 = (f32[32]{0:T(128)S(1)}, f32[32]{0:T(128)}, u32[]{:S(2)}) copy-start(f32[32]{0:T(128)} %param.6) | copy-start | bytes 388
  0.0 0.7 %copy-start.2 = (s32[31]{0:T(128)S(1)}, s32[31]{0:T(128)}, u32[]{:S(2)}) copy-start(s32[31]{0:T(128)} %param.7) | copy-start | bytes 376

commit v7 on v4

--- a/solution.py
+++ b/solution.py
@@ -251,13 +251,17 @@
             def _():
                 spread_near(j)
 
-            @pl.when((j + 2) // 4 == 2)
+            far = u // 2
+            k_of = (part, part, (0, 1, 0, 2)[part], (1, 3, 2, 3)[part])
+            mate_of = (0, 1, (0, 0, 1, 0)[part], (1, 0, 1, 1)[part])
+            unit = (1 + 3 * (u % 2)) * (1 + 15 * (u // 2))
+            k = sum(v * 4**i for i, v in enumerate(k_of)) // unit % 4
+            mate = sum(v * 4**i for i, v in enumerate(mate_of)) // unit % 4
+
+            @pl.when((far == 1) & (mate == 0))
             def _():
-                spread_far(j - 6)
-
-            far = j // 8
-            mate = (1 - far) * (j // 4 % 2) + far * (j // 2 % 2)
-            k = (1 - far) * (j % 4) + far * (j % 8 // 4 * 2 + j % 2)
+                spread_far(k)
+
             hh = place(along_z(k), (y + far) % 2, (c + mate) % 2)
 
             @pl.when(mate == 1)

time: 26.7 us -> 26.1 us (0.978)
  Pallas kernels: 25 us -> 24.4 us
    pallas_call x1, Pallas kernels: 25 us -> 24.4 us  [on_slice(): pl.pallas_call(gram_kernel, out_shape=jax.ShapeDtypeStruct((136, 1088), j...]
where the time goes in v7:
time: 26.1 us; the launch traced here: 25.9 us
  Pallas kernels  24.4 us (93%)
  local copies, waits for them, and re-layouts  1.51 us (6%)
    pallas_call x1, Pallas kernels, on_slice(): pl.pallas_call(gram_kernel, out_shape=jax.ShapeDtypeStruct((136, 1088), j...  24.4 us
    unnamed x7, local copies, waits for them, and re-layouts  1.51 us

profile of v7, /device:TPU:0, one launch (start us, length us, event | category | flops | bytes accessed | tf_op | source)
XLA Modules:
  0.0 25.9 jit_solution(9962647675884600110)
XLA Ops:
  0.0 0.0 copy-start
  0.0 0.0 copy-start.1
  0.0 0.0 copy-start.2
  0.0 0.6 %copy-done = s32[1,128]{1,0:T(1,128)S(1)} copy-done((s32[1,128]{1,0:T(1,128)S(1)}, s32[1,128]{1,0:T(1,128)}, u32[]{:S(2)}) %copy-start) | copy-done | bytes 536
  0.7 0.0 copy-done.1
  0.7 0.0 copy-done.2
  0.7 24.4 %shard_map.46 = f32[136,1088]{1,0:T(8,128)S(1)} custom-call(f32[4,16,4096]{2,1,0:T(8,128)} %slab_hbm.1, s32[1,128]{1,0:T(1,128)S(1)} %copy-done, f32[1,32]{1,0:T(1,128)S(1)} %bitcast.2, s32[1,31]{1,0:T(1,128)S(1)} %bitcast.3), custom_call_target="tpu_custom_call" | custom-call | tf_op jit(solution)/shard_map/pallas_call | solution.py:287
  25.1 0.8 %copy.6 = f32[136,1088]{1,0:T(8,128)} copy(f32[136,1088]{1,0:T(8,128)S(1)} %shard_map.46) | data formatting | bytes 1183744
Async XLA Ops:
  0.0 0.7 %copy-start = (s32[1,128]{1,0:T(1,128)S(1)}, s32[1,128]{1,0:T(1,128)}, u32[]{:S(2)}) copy-start(s32[1,128]{1,0:T(1,128)} %idx_hbm.1) | copy-start | bytes 1540
  0.0 0.7 %copy-start.1 = (f32[32]{0:T(128)S(1)}, f32[32]{0:T(128)}, u32[]{:S(2)}) copy-start(f32[32]{0:T(128)} %param.6) | copy-start | bytes 388
  0.0 0.7 %copy-start.2 = (s32[31]{0:T(128)S(1)}, s32[31]{0:T(128)}, u32[]{:S(2)}) copy-start(s32[31]{0:T(128)} %param.7) | copy-start | bytes 376

commit v8 on v7

--- a/solution.py
+++ b/solution.py
@@ -145,10 +145,6 @@
     idx_load.wait()
     own_load.wait()
     pick(x, idx_ref[...])
-    other_load.wait()
-    idx_copy.wait_recv()
-    pick(1 - x, other_idx[...])
-
     thick_load.wait()
     cuts_load.wait()
 
@@ -168,6 +164,10 @@
     denom = weights[0] + weights[1] + weights[2]
     for i in range(3):
         coef_ref[i] = jnp.broadcast_to(weights[i] / denom, (32, 128))
+
+    other_load.wait()
+    idx_copy.wait_recv()
+    pick(1 - x, other_idx[...])
 
     def forward_z(i, carry):
         g = (x + i) % 2

time: 26.1 us -> 26.1 us (level)
  no operation moved by 1% of the time
where the time goes in v8:
time: 26.1 us; the launch traced here: 25.9 us
  Pallas kernels  24.4 us (93%)
  local copies, waits for them, and re-layouts  1.51 us (6%)
    pallas_call x1, Pallas kernels, on_slice(): pl.pallas_call(gram_kernel, out_shape=jax.ShapeDtypeStruct((136, 1088), j...  24.4 us
    unnamed x7, local copies, waits for them, and re-layouts  1.51 us

profile of v8, /device:TPU:0, one launch (start us, length us, event | category | flops | bytes accessed | tf_op | source)
XLA Modules:
  0.0 25.9 jit_solution(6317985062271551104)
XLA Ops:
  0.0 0.0 copy-start
  0.0 0.0 copy-start.1
  0.0 0.0 copy-start.2
  0.0 0.6 %copy-done = s32[1,128]{1,0:T(1,128)S(1)} copy-done((s32[1,128]{1,0:T(1,128)S(1)}, s32[1,128]{1,0:T(1,128)}, u32[]{:S(2)}) %copy-start) | copy-done | bytes 536
  0.7 0.0 copy-done.1
  0.7 0.0 copy-done.2
  0.7 24.4 %shard_map.46 = f32[136,1088]{1,0:T(8,128)S(1)} custom-call(f32[4,16,4096]{2,1,0:T(8,128)} %slab_hbm.1, s32[1,128]{1,0:T(1,128)S(1)} %copy-done, f32[1,32]{1,0:T(1,128)S(1)} %bitcast.2, s32[1,31]{1,0:T(1,128)S(1)} %bitcast.3), custom_call_target="tpu_custom_call" | custom-call | tf_op jit(solution)/shard_map/pallas_call | solution.py:287
  25.1 0.8 %copy.6 = f32[136,1088]{1,0:T(8,128)} copy(f32[136,1088]{1,0:T(8,128)S(1)} %shard_map.46) | data formatting | bytes 1183744
Async XLA Ops:
  0.0 0.7 %copy-start = (s32[1,128]{1,0:T(1,128)S(1)}, s32[1,128]{1,0:T(1,128)}, u32[]{:S(2)}) copy-start(s32[1,128]{1,0:T(1,128)} %idx_hbm.1) | copy-start | bytes 1540
  0.0 0.7 %copy-start.1 = (f32[32]{0:T(128)S(1)}, f32[32]{0:T(128)}, u32[]{:S(2)}) copy-start(f32[32]{0:T(128)} %param.6) | copy-start | bytes 388
  0.0 0.7 %copy-start.2 = (s32[31]{0:T(128)S(1)}, s32[31]{0:T(128)}, u32[]{:S(2)}) copy-start(s32[31]{0:T(128)} %param.7) | copy-start | bytes 376
